TPU v7x, 32 devices: a whole 2x2x4 slice. The times are simulated.
32 devices in a mesh: load: 4 (over z), tile: 8 (over y, x, core).
Axes of the slice: x: 2, y: 2, z: 4, core: 2. Of those that a mesh axis runs over, the one named last changes fastest.
Arguments:
- u_prev: float32 [4, 3, 64, 16, 128], P('load', None, 'tile'), may hold values from -0.5 to 0.5
- density: float32 [64, 16, 128], P('tile'), may hold values from 0.3 to 1
- active_blocks: int32 [8, 2, 16], P('tile'), may hold values 0 or 1
- fixed_nodes: int32 [64, 16, 128], P('tile'), may hold values 0 or 1
- load_nodes: int32 [4, 32], P('load'), may hold values from 0 to 131071
- load_forces: float32 [4, 3, 32], P('load'), may hold values from -5 to 5
Outputs:
- displacement: float32 [4, 3, 64, 16, 128], P('load', None, 'tile')
- sensitivity: float32 [64, 16, 128], P('tile')
All inputs are finite; a program needn't handle non-finite values. No bound on the sum of `active_blocks` or of `fixed_nodes` on one device may be relied on, other than what follows from the above.
Results may differ from a plain program's by a relative error of at most 0.0003.
Values sent between devices are 32-bit elements; how exact they have to be, the bound alone decides.
A program may use at most 64 MiB of HBM per device.

v0:
```python
import math

import jax
import jax.numpy as jnp
import numpy as np
from jax import lax
from jax.sharding import PartitionSpec as P

ITERS = 2
BLOCK = 8


def shifted(array, axis, by):
    length = lax.axis_size(axis)
    pairs = [(i, i + by) for i in range(length) if 0 <= i + by < length]
    return lax.ppermute(array, axis, pairs)


def stiffness_table():
    poisson = 0.3
    lame_first = poisson / ((1.0 + poisson) * (1.0 - 2.0 * poisson))
    shear_modulus = 0.5 / (1.0 + poisson)
    elastic = np.zeros((6, 6))
    elastic[:3, :3] = lame_first
    for component in range(3):
        elastic[component, component] += 2.0 * shear_modulus
        elastic[component + 3, component + 3] = shear_modulus
    gauss_points = [0.5 - 0.5 / math.sqrt(3.0), 0.5 + 0.5 / math.sqrt(3.0)]
    stiffness = np.zeros((24, 24))
    for point_x in gauss_points:
        for point_y in gauss_points:
            for point_z in gauss_points:
                strain = np.zeros((6, 24))
                for corner in range(8):
                    bit_x = corner & 1
                    bit_y = corner >> 1 & 1
                    bit_z = corner >> 2 & 1
                    shape_x = point_x if bit_x == 1 else 1.0 - point_x
                    shape_y = point_y if bit_y == 1 else 1.0 - point_y
                    shape_z = point_z if bit_z == 1 else 1.0 - point_z
                    slope_x = 1.0 if bit_x == 1 else -1.0
                    slope_y = 1.0 if bit_y == 1 else -1.0
                    slope_z = 1.0 if bit_z == 1 else -1.0
                    grad_x = slope_x * shape_y * shape_z
                    grad_y = shape_x * slope_y * shape_z
                    grad_z = shape_x * shape_y * slope_z
                    column = 3 * corner
                    strain[0, column] = grad_x
                    strain[1, column + 1] = grad_y
                    strain[2, column + 2] = grad_z
                    strain[3, column + 1] = grad_z
                    strain[3, column + 2] = grad_y
                    strain[4, column] = grad_z
                    strain[4, column + 2] = grad_x
                    strain[5, column] = grad_y
                    strain[5, column + 1] = grad_x
                stiffness += 0.125 * strain.T @ elastic @ strain
    return stiffness.astype(np.float32)


def corner_bits(corner):
    return (corner & 1, corner >> 1 & 1, corner >> 2 & 1)


def stacked_corners(widened):
    planes = widened.shape[1] - 1
    size_y = widened.shape[2]
    size_z = widened.shape[3]
    padded = jnp.pad(widened, ((0, 0), (0, 0), (0, 1), (0, 1)))
    pieces = []
    for corner in range(8):
        bit_x, bit_y, bit_z = corner_bits(corner)
        pieces.append(
            padded[:, bit_x : bit_x + planes, bit_y : bit_y + size_y, bit_z : bit_z + size_z]
        )
    return jnp.concatenate(pieces, axis=0)


def spread_corner(values, corner):
    bit_x, bit_y, bit_z = corner_bits(corner)
    padded = jnp.pad(values, ((0, 0), (bit_x, 1 - bit_x), (bit_y, 1 - bit_y), (bit_z, 1 - bit_z)))
    return padded[:, :, :-1, :-1]


def element_forces(stacked):
    matrix = jnp.asarray(stiffness_table())
    flat = stacked.reshape(24, -1)
    forces = jnp.dot(
        matrix, flat, precision=lax.Precision.HIGHEST, preferred_element_type=jnp.float32
    )
    return forces.reshape(stacked.shape)


def apply_element(widened, weight):
    forces = element_forces(stacked_corners(widened)) * weight[None]
    summed = None
    for target in range(8):
        term = spread_corner(forces[3 * target : 3 * target + 3], target)
        summed = term if summed is None else summed + term
    return summed


def diagonal_sum(weight):
    stiffness = stiffness_table()
    summed = None
    for target in range(8):
        entries = [float(stiffness[3 * target + c, 3 * target + c]) for c in range(3)]
        column = jnp.asarray(entries, dtype=jnp.float32).reshape(3, 1, 1, 1)
        term = spread_corner(column * weight[None], target)
        summed = term if summed is None else summed + term
    return summed


def element_energy(widened):
    stacked = stacked_corners(widened)
    return jnp.sum(stacked * element_forces(stacked), axis=0)


def residual_sum(residual, precond):
    return lax.psum(jnp.sum(residual * precond), "tile")


def shards(u_prev, density, active_blocks, fixed_nodes, load_nodes, load_forces):
    planes = density.shape[0]
    size_y = density.shape[1]
    size_z = density.shape[2]
    block_x = active_blocks.shape[0]
    block_y = active_blocks.shape[1]
    block_z = active_blocks.shape[2]
    grown = jnp.broadcast_to(
        active_blocks[:, None, :, None, :, None], (block_x, BLOCK, block_y, BLOCK, block_z, BLOCK)
    )
    active = (grown.reshape(planes, size_y, size_z) == 1).astype(jnp.float32)
    weight = density * density * density * active

    def widen_nodes(node_field):
        following = shifted(node_field[:, :1], "tile", -1)
        return jnp.concatenate([node_field, following], axis=1)

    def narrow_nodes(summed):
        returned = shifted(summed[:, planes : planes + 1], "tile", 1)
        return summed[:, :planes] + jnp.pad(returned, ((0, 0), (0, planes - 1), (0, 0), (0, 0)))

    diagonal = narrow_nodes(diagonal_sum(weight))
    free_mask = ((fixed_nodes[None] == 0) & (diagonal > 0.0)).astype(jnp.float32)
    inverse = free_mask / (diagonal + 1.0 - free_mask)

    def operate(vector):
        return free_mask * narrow_nodes(apply_element(widen_nodes(vector), weight))

    plane_size = size_y * size_z
    offset = lax.axis_index("tile") * (planes * plane_size)
    local_ids = load_nodes[0] - offset
    inside = (local_ids >= 0) & (local_ids < planes * plane_size)
    safe_ids = jnp.where(inside, local_ids, 0)
    placed = load_forces[0] * inside.astype(jnp.float32)[None, :]
    force_field = jnp.zeros((3, planes * plane_size), jnp.float32).at[:, safe_ids].add(placed)
    force_field = force_field.reshape(3, planes, size_y, size_z)
    solution = free_mask * u_prev[0]
    residual = free_mask * force_field - operate(solution)
    precond = inverse * residual
    direction = precond
    inner_now = residual_sum(residual, precond)
    for iteration in range(ITERS):
        applied = operate(direction)
        curvature = lax.psum(jnp.sum(direction * applied), "tile")
        step_size = inner_now / curvature
        solution = solution + step_size * direction
        residual = residual - step_size * applied
        if iteration + 1 < ITERS:
            precond = inverse * residual
            inner_next = residual_sum(residual, precond)
            direction = precond + inner_next / inner_now * direction
            inner_now = inner_next
    widened = widen_nodes(solution)
    energy = element_energy(widened)
    own_terms = -3.0 / lax.axis_size("load") * density * density * active * energy
    sensitivity = lax.psum(own_terms, "load")
    return (solution[None], sensitivity)


def solution(mesh):
    in_specs = (
        P("load", None, "tile", None, None),
        P("tile", None, None),
        P("tile", None, None),
        P("tile", None, None),
        P("load", None),
        P("load", None, None),
    )
    out_specs = (P("load", None, "tile", None, None), P("tile", None, None))
    return jax.shard_map(shards, mesh=mesh, in_specs=in_specs, out_specs=out_specs, check_vma=False)
```

profile of v0, /device:TPU:0, one launch (start us, length us, event | category | flops | bytes accessed | tf_op | source)
XLA Modules:
  0.0 175.7 jit_solution(15953622748213115061)
XLA Ops:
  9.3 2.4 %collective-permute-start = (f32[3,1,16,128]{3,2,1,0:T(8,128)S(1)}, f32[3,1,16,128]{3,2,1,0:T(8,128)S(1)}, u32[]{:S(2)}, u32[]{:S(2)}) collective-permute-start(f32[3,1,16,128]{3,2,1,0:T(8,128)S(1)} %slice.397), channel_id=1, source_target_pairs={{0,1},{1,2},{2,3},{3,4},{4,5},{5,6},{6,7},{8,9},{9,10},{10,11},{11... | collective-permute-start | bytes 73736 | tf_op jit(solution)/shard_map/ppermute | solution.py:16
  14.2 1.3 collective-permute-start.1
  15.5 3.9 %collective-permute-done.1 = f32[3,1,16,128]{3,2,1,0:T(8,128)S(1)} collective-permute-done((f32[3,1,16,128]{3,2,1,0:T(8,128)S(1)}, f32[3,1,16,128]{3,2,1,0:T(8,128)S(1)}, u32[]{:S(2)}, u32[]{:S(2)}) %collective-permute-start.1) | collective-permute-done | bytes 24608 | tf_op jit(solution)/shard_map/ppermute | solution.py:16
  20.1 2.2 %fusion.13 = f32[3,8,128,128]{3,1,2,0:T(8,128)S(1)} fusion(f32[24,24]{1,0:T(8,128)S(1)} %copy-done.2, f32[3,8,128,128]{3,2,1,0:T(8,128)S(1)} %bitcast.107), kind=kOutput, calls=%fused_computation.39 | convolution fusion | flops 113246208 | bytes 3148032 | tf_op jit(solution)/shard_map/dot_general | solution.py:88
  23.1 4.5 %collective-permute-start.2 = (f32[3,1,16,128]{3,2,1,0:T(8,128)S(1)}, f32[3,1,16,128]{3,2,1,0:T(8,128)S(1)}, u32[]{:S(2)}, u32[]{:S(2)}) collective-permute-start(f32[3,1,16,128]{3,2,1,0:T(8,128)S(1)} %slice.410), channel_id=1, source_target_pairs={{0,1},{1,2},{2,3},{3,4},{4,5},{5,6},{6,7},{8,9},{9,10},{10,11},{11... | collective-permute-start | bytes 73736 | tf_op jit(solution)/shard_map/ppermute | solution.py:16
  27.7 4.5 %scatter_custom_fusion = f32[3,16384]{0,1:T(8,128)} fusion(s32[32]{0:T(128)S(1)} %fusion.89, f32[32,3]{1,0:T(8,128)S(1)} %copy.22, f32[]{:T(128)} %constant.13.clone.1), kind=kCustom, calls=%fused_computation.2 | custom fusion | flops 96 | bytes 196612 | tf_op jit(solution)/shard_map/scatter-add | solution.py:157
  32.2 5.2 %copy.23 = f32[3,8,16,128]{3,2,1,0:T(8,128)S(1)} copy(f32[3,8,16,128]{0,3,2,1:T(8,128)} %bitcast.100) | data formatting | bytes 393216 | tf_op jit(solution)/shard_map/reshape | solution.py:158
  37.6 1.3 collective-permute-start.3
  38.9 1.8 %collective-permute-done.3 = f32[3,1,16,128]{3,2,1,0:T(8,128)S(1)} collective-permute-done((f32[3,1,16,128]{3,2,1,0:T(8,128)S(1)}, f32[3,1,16,128]{3,2,1,0:T(8,128)S(1)}, u32[]{:S(2)}, u32[]{:S(2)}) %collective-permute-start.3) | collective-permute-done | bytes 24608 | tf_op jit(solution)/shard_map/ppermute | solution.py:16
  41.2 2.2 %fusion.16 = f32[3,8,128,128]{3,1,2,0:T(8,128)S(1)} fusion(f32[24,24]{1,0:T(8,128)S(1)} %copy-done.2, f32[3,8,128,128]{3,2,1,0:T(8,128)S(1)} %bitcast.108), kind=kOutput, calls=%fused_computation.40 | convolution fusion | flops 113246208 | bytes 3148032 | tf_op jit(solution)/shard_map/dot_general | solution.py:88
  44.2 4.7 %collective-permute-start.4 = (f32[3,1,16,128]{3,2,1,0:T(8,128)S(1)}, f32[3,1,16,128]{3,2,1,0:T(8,128)S(1)}, u32[]{:S(2)}, u32[]{:S(2)}) collective-permute-start(f32[3,1,16,128]{3,2,1,0:T(8,128)S(1)} %slice.423), channel_id=1, source_target_pairs={{0,1},{1,2},{2,3},{3,4},{4,5},{5,6},{6,7},{8,9},{9,10},{10,11},{11... | collective-permute-start | bytes 73736 | tf_op jit(solution)/shard_map/ppermute | solution.py:16
  50.5 12.8 %all-reduce.40 = (f32[]{:T(128)}, f32[]{:T(128)}) all-reduce(f32[]{:T(128)} %get-tuple-element.3, f32[]{:T(128)} %get-tuple-element.2), channel_id=1, replica_groups=mesh['load'=4,'tile'=8] {'tile'}, use_global_device_ids=true, to_apply=%region_2.3 | all-reduce | flops 2 | bytes 16 | tf_op jit(solution)/shard_map/psum | solution.py:120
  65.3 14.1 %psum.37 = f32[]{:T(128)} all-reduce(f32[]{:T(128)} %multiply_reduce_fusion), channel_id=1, replica_groups=mesh['load'=4,'tile'=8] {'tile'}, use_global_device_ids=true, to_apply=%region_6.7 | all-reduce | flops 1 | bytes 8 | tf_op jit(solution)/shard_map/psum | solution.py:120
  80.9 1.5 collective-permute-start.5
  82.4 1.6 collective-permute-done.5
  84.6 2.2 %fusion.19 = f32[3,8,128,128]{3,1,2,0:T(8,128)S(1)} fusion(f32[24,24]{1,0:T(8,128)S(1)} %copy-done.2, f32[3,8,128,128]{3,2,1,0:T(8,128)S(1)} %bitcast.109), kind=kOutput, calls=%fused_computation.41 | convolution fusion | flops 113246208 | bytes 3148032 | tf_op jit(solution)/shard_map/dot_general | solution.py:88
  87.6 2.4 %collective-permute-start.6 = (f32[3,1,16,128]{3,2,1,0:T(8,128)S(1)}, f32[3,1,16,128]{3,2,1,0:T(8,128)S(1)}, u32[]{:S(2)}, u32[]{:S(2)}) collective-permute-start(f32[3,1,16,128]{3,2,1,0:T(8,128)S(1)} %slice.436), channel_id=1, source_target_pairs={{0,1},{1,2},{2,3},{3,4},{4,5},{5,6},{6,7},{8,9},{9,10},{10,11},{11... | collective-permute-start | bytes 73736 | tf_op jit(solution)/shard_map/ppermute | solution.py:16
  91.5 15.4 %psum.38 = f32[]{:T(128)} all-reduce(f32[]{:T(128)} %fusion.80), channel_id=1, replica_groups=mesh['load'=4,'tile'=8] {'tile'}, use_global_device_ids=true, to_apply=%region_8.9 | all-reduce | flops 1 | bytes 8 | tf_op jit(solution)/shard_map/psum | solution.py:166
  108.2 1.3 collective-permute-start.7
  114.0 1.1 copy_bitcast_fusion.2
  116.2 11.3 %concatenate.58 = f32[24,16384]{1,0:T(8,128)S(1)} concatenate(f32[3,16384]{1,0:T(4,128)} %bitcast.110, f32[3,16384]{1,0:T(4,128)} %bitcast.111, f32[3,16384]{1,0:T(4,128)} %get-tuple-element.56, f32[3,16384]{1,0:T(4,128)} %get-tuple-element.55, f32[3,16384]{1,0:T(4,128)} %get-tuple-element.54, f32[3,16384]{1,0:T(4,128)} %get-tuple-element.53, f32[3,16384]{1,0:T(4,128)} %get-tuple-element.52, ...), dimensions={0} | concatenate | bytes 3145728 | tf_op jit(solution)/shard_map/concatenate | solution.py:76
  127.5 2.3 %fusion.22 = f32[16384]{0:T(1024)S(1)} fusion(f32[24,16384]{1,0:T(8,128)S(1)} %concatenate.58, f32[24,24]{1,0:T(8,128)S(1)} %copy-done.2, f32[3,8,128,128]{3,2,1,0:T(8,128)S(1)} %bitcast.106), kind=kOutput, calls=%fused_computation.42 | convolution fusion | flops 114016256 | bytes 3213568 | tf_op jit(solution)/shard_map/dot_general | solution.py:88
  130.5 37.0 %all-reduce.43.cloned.1.call-done = f32[8,16,128]{2,1,0:T(8,128)} async-done(((f32[8,16,128]{2,1,0:T(8,128)}), f32[8,16,128]{2,1,0:T(8,128)}) %all-reduce.43.cloned.1.call-update) | async-done | bytes 65552 | tf_op jit(solution)/shard_map/psum | solution.py:178
  167.4 1.5 copy.104
  (92 shorter events, 18.9 us)
Async XLA Ops:
  7.2 8.3 %copy-start.3 = (f32[1,3,32]{2,0,1:T(1,128)S(1)}, f32[1,3,32]{2,0,1:T(1,128)}, u32[]{:S(2)}) copy-start(f32[1,3,32]{2,0,1:T(1,128)} %param.23) | copy-start | bytes 1156
  7.2 160.3 %all-reduce.43.cloned.1.call-start = ((), (), s32[]{:S(2)}) async-start(), calls=%async_computation | async-start | bytes 131072 | tf_op jit(solution)/shard_map/psum | solution.py:178
  9.3 3.9 %collective-permute-start = (f32[3,1,16,128]{3,2,1,0:T(8,128)S(1)}, f32[3,1,16,128]{3,2,1,0:T(8,128)S(1)}, u32[]{:S(2)}, u32[]{:S(2)}) collective-permute-start(f32[3,1,16,128]{3,2,1,0:T(8,128)S(1)} %slice.397), channel_id=1, source_target_pairs={{0,1},{1,2},{2,3},{3,4},{4,5},{5,6},{6,7},{8,9},{9,10},{10,11},{11... | collective-permute-start | bytes 73736 | tf_op jit(solution)/shard_map/ppermute | solution.py:16
  14.2 5.2 %collective-permute-start.1 = (f32[3,1,16,128]{3,2,1,0:T(8,128)S(1)}, f32[3,1,16,128]{3,2,1,0:T(8,128)S(1)}, u32[]{:S(2)}, u32[]{:S(2)}) collective-permute-start(f32[3,1,16,128]{3,2,1,0:T(8,128)S(1)} %slice.398), channel_id=1, source_target_pairs={{1,0},{2,1},{3,2},{4,3},{5,4},{6,5},{7,6},{9,8},{10,9},{11,10},{12... | collective-permute-start | bytes 73736 | tf_op jit(solution)/shard_map/ppermute | solution.py:16
  19.4 0.7 copy-start.2
  22.8 4.8 %copy-start.4 = (s32[1,32]{1,0:T(1,128)S(1)}, s32[1,32]{1,0:T(1,128)}, u32[]{:S(2)}) copy-start(s32[1,32]{1,0:T(1,128)} %param.22) | copy-start | bytes 388
  23.1 14.3 %collective-permute-start.2 = (f32[3,1,16,128]{3,2,1,0:T(8,128)S(1)}, f32[3,1,16,128]{3,2,1,0:T(8,128)S(1)}, u32[]{:S(2)}, u32[]{:S(2)}) collective-permute-start(f32[3,1,16,128]{3,2,1,0:T(8,128)S(1)} %slice.410), channel_id=1, source_target_pairs={{0,1},{1,2},{2,3},{3,4},{4,5},{5,6},{6,7},{8,9},{9,10},{10,11},{11... | collective-permute-start | bytes 73736 | tf_op jit(solution)/shard_map/ppermute | solution.py:16
  37.6 3.1 %collective-permute-start.3 = (f32[3,1,16,128]{3,2,1,0:T(8,128)S(1)}, f32[3,1,16,128]{3,2,1,0:T(8,128)S(1)}, u32[]{:S(2)}, u32[]{:S(2)}) collective-permute-start(f32[3,1,16,128]{3,2,1,0:T(8,128)S(1)} %slice.411), channel_id=1, source_target_pairs={{1,0},{2,1},{3,2},{4,3},{5,4},{6,5},{7,6},{9,8},{10,9},{11,10},{12... | collective-permute-start | bytes 73736 | tf_op jit(solution)/shard_map/ppermute | solution.py:16
  44.2 5.5 %collective-permute-start.4 = (f32[3,1,16,128]{3,2,1,0:T(8,128)S(1)}, f32[3,1,16,128]{3,2,1,0:T(8,128)S(1)}, u32[]{:S(2)}, u32[]{:S(2)}) collective-permute-start(f32[3,1,16,128]{3,2,1,0:T(8,128)S(1)} %slice.423), channel_id=1, source_target_pairs={{0,1},{1,2},{2,3},{3,4},{4,5},{5,6},{6,7},{8,9},{9,10},{10,11},{11... | collective-permute-start | bytes 73736 | tf_op jit(solution)/shard_map/ppermute | solution.py:16
  80.9 3.1 %collective-permute-start.5 = (f32[3,1,16,128]{3,2,1,0:T(8,128)S(1)}, f32[3,1,16,128]{3,2,1,0:T(8,128)S(1)}, u32[]{:S(2)}, u32[]{:S(2)}) collective-permute-start(f32[3,1,16,128]{3,2,1,0:T(8,128)S(1)} %slice.424), channel_id=1, source_target_pairs={{1,0},{2,1},{3,2},{4,3},{5,4},{6,5},{7,6},{9,8},{10,9},{11,10},{12... | collective-permute-start | bytes 73736 | tf_op jit(solution)/shard_map/ppermute | solution.py:16
  87.6 3.2 %collective-permute-start.6 = (f32[3,1,16,128]{3,2,1,0:T(8,128)S(1)}, f32[3,1,16,128]{3,2,1,0:T(8,128)S(1)}, u32[]{:S(2)}, u32[]{:S(2)}) collective-permute-start(f32[3,1,16,128]{3,2,1,0:T(8,128)S(1)} %slice.436), channel_id=1, source_target_pairs={{0,1},{1,2},{2,3},{3,4},{4,5},{5,6},{6,7},{8,9},{9,10},{10,11},{11... | collective-permute-start | bytes 73736 | tf_op jit(solution)/shard_map/ppermute | solution.py:16
  108.2 4.2 %copy-start = (f32[3,8,16,128]{3,2,1,0:T(8,128)}, f32[3,8,16,128]{3,2,1,0:T(8,128)S(1)}, u32[]{:S(2)}) copy-start(f32[3,8,16,128]{3,2,1,0:T(8,128)S(1)} %get-tuple-element.9) | copy-start | bytes 589828
  108.2 3.1 %collective-permute-start.7 = (f32[3,1,16,128]{3,2,1,0:T(8,128)S(1)}, f32[3,1,16,128]{3,2,1,0:T(8,128)S(1)}, u32[]{:S(2)}, u32[]{:S(2)}) collective-permute-start(f32[3,1,16,128]{3,2,1,0:T(8,128)S(1)} %slice.437), channel_id=1, source_target_pairs={{1,0},{2,1},{3,2},{4,3},{5,4},{6,5},{7,6},{9,8},{10,9},{11,10},{12... | collective-permute-start | bytes 73736 | tf_op jit(solution)/shard_map/ppermute | solution.py:16
  127.5 2.3 %copy-start.1 = (f32[8,16,128]{2,1,0:T(8,128)S(1)}, f32[8,16,128]{2,1,0:T(8,128)}, u32[]{:S(2)}) copy-start(f32[8,16,128]{2,1,0:T(8,128)} %param.19) | copy-start | bytes 196612
Sparse Core Ops, SparseCore 0:
  130.6 36.7 all-reduce.42
where the time goes:
time: 177 us; the launch traced here: 176 us
  waiting for transfers between devices  46.9 us (26%)
  blocking collectives  42.3 us (24%)
  local copies, waits for them, and re-layouts  26.7 us (15%)
  starting transfers between devices  19.3 us (11%)
  between operations  18.7 us (11%)
  other arithmetic  13.2 us (7%)
  matrix products  8.76 us (5%)
    psum x1, waiting for transfers between devices, shards(): sensitivity = lax.psum(own_terms, 'load')  37 us
    psum x2, blocking collectives, residual_sum(): return lax.psum(jnp.sum(residual * precond), 'tile')  26.9 us
    ppermute x8, starting transfers between devices, shifted(): return lax.ppermute(array, axis, pairs)  19.3 us
    psum x1, blocking collectives, shards(): curvature = lax.psum(jnp.sum(direction * applied), 'tile')  15.4 us
    concatenate x8, local copies, waits for them, and re-layouts, stacked_corners(): return jnp.concatenate(pieces, axis=0)  15.2 us
    ppermute x8, waiting for transfers between devices, shifted(): return lax.ppermute(array, axis, pairs)  9.9 us
    dot_general x4, matrix products, element_forces(): jnp.dot(matrix, flat, precision=lax.Precision.HIGHEST, preferred_element_...  8.76 us
    unnamed x36, local copies, waits for them, and re-layouts  5.61 us
  transfers between devices with their start and end apart: 9, of which 7 were waited for; matrix products, arithmetic and copies ran while one was open for 7% of the time, Pallas kernels for 0%

commit v1 on v0

v1 whole, which is shorter than its diff:
```python
import functools

import jax
import jax.numpy as jnp
from jax import lax
from jax.experimental import pallas as pl
from jax.experimental.pallas import tpu as pltpu
from jax.sharding import PartitionSpec as P

BLOCK = 8
DEEP = 3
CHUNK = 1
POISSON = 0.3
LAM = POISSON / ((1.0 + POISSON) * (1.0 - 2.0 * POISSON))
MU = 0.5 / (1.0 + POISSON)
DIAG = (LAM + 4.0 * MU) / 9.0
MESH = pl.DeviceIdType.MESH


def up(array, axis):
    size = array.shape[axis]
    spot = lax.broadcasted_iota(jnp.int32, array.shape, axis)
    return jnp.where(spot == size - 1, 0.0, pltpu.roll(array, size - 1, axis))


def down(array, axis):
    spot = lax.broadcasted_iota(jnp.int32, array.shape, axis)
    return jnp.where(spot == 0, 0.0, pltpu.roll(array, 1, axis))


def flat_modes(plane):
    above = up(plane, 2)
    modes = {}
    for key, part in (("S", plane + above), ("D", above - plane)):
        beyond = up(part, 1)
        modes["S" + key] = part + beyond
        modes["D" + key] = beyond - part
    return modes


def cube_modes(low, high):
    modes = []
    for first, second in zip(low, high):
        own = {}
        for key in first:
            if key != "SS":
                own["S" + key] = first[key] + second[key]
            own["D" + key] = second[key] - first[key]
        modes.append(own)
    return modes


def mode_forces(modes, weight):
    u, v, w = modes
    first, middle, last = weight * (1.0 / 16.0), weight * (1.0 / 48.0), weight * ((LAM + 4.0 * MU) / 144.0)
    fu, fv, fw = {}, {}, {}
    trace = LAM * (u["DSS"] + v["SDS"] + w["SSD"])
    fu["DSS"] = first * (trace + 2.0 * MU * u["DSS"])
    fv["SDS"] = first * (trace + 2.0 * MU * v["SDS"])
    fw["SSD"] = first * (trace + 2.0 * MU * w["SSD"])
    for one, other, fone, fother, ka, kb in (
        (u, w, fu, fw, "DDS", "SDD"),
        (v, w, fv, fw, "DDS", "DSD"),
        (u, v, fu, fv, "DSD", "SDD"),
    ):
        trace = LAM * (one[ka] + other[kb])
        fone[ka] = middle * (trace + 3.0 * MU * one[ka])
        fother[kb] = middle * (trace + 3.0 * MU * other[kb])
    fu["DDD"] = last * u["DDD"]
    fv["DDD"] = last * v["DDD"]
    fw["DDD"] = last * w["DDD"]
    shear = first * MU
    fu["SDS"] = fv["DSS"] = shear * (u["SDS"] + v["DSS"])
    fu["SSD"] = fw["DSS"] = shear * (u["SSD"] + w["DSS"])
    fv["SSD"] = fw["SDS"] = shear * (v["SSD"] + w["SDS"])
    bend = middle * MU
    total = u["SDD"] + v["DSD"] + w["DDS"]
    fu["SDD"] = bend * (total + u["SDD"])
    fv["DSD"] = bend * (total + v["DSD"])
    fw["DDS"] = bend * (total + w["DDS"])
    return fu, fv, fw


def mode_energy(modes):
    u, v, w = modes

    def sq(x):
        return x * x

    first = LAM * sq(u["DSS"] + v["SDS"] + w["SSD"]) + 2.0 * MU * (sq(u["DSS"]) + sq(v["SDS"]) + sq(w["SSD"]))
    first = first + MU * (sq(u["SDS"] + v["DSS"]) + sq(u["SSD"] + w["DSS"]) + sq(v["SSD"] + w["SDS"]))
    pairs = ((u["DDS"], w["SDD"]), (v["DDS"], w["DSD"]), (u["DSD"], v["SDD"]))
    traces = sum(sq(a + b) for a, b in pairs)
    squares = sum(sq(a) + sq(b) for a, b in pairs)
    a, b, c = u["SDD"], v["DSD"], w["DDS"]
    middle = LAM * traces + 3.0 * MU * squares + MU * (sq(a + b) + sq(a + c) + sq(b + c))
    last = (LAM + 4.0 * MU) * (sq(u["DDD"]) + sq(v["DDD"]) + sq(w["DDD"]))
    return first * (1.0 / 16.0) + middle * (1.0 / 48.0) + last * (1.0 / 144.0)


def spread(modes):
    along = {}
    for key in "SD":
        total, delta = modes["S" + key], modes["D" + key]
        along[key] = (total - delta) + down(total + delta, 1)
    return (along["S"] - along["D"]) + down(along["S"] + along["D"], 2)


def stiffness(planes_of, weight_of, store, count):
    low = [flat_modes(field) for field in planes_of(0)]
    carry = None
    for element in range(count):
        high = [flat_modes(field) for field in planes_of(element + 1)]
        forces = mode_forces(cube_modes(low, high), weight_of(element))
        lower, upper = [], []
        for force in forces:
            lower.append({k: force["S" + k] - force["D" + k] if k != "SS" else -force["D" + k] for k in ("SS", "SD", "DS", "DD")})
            upper.append({k: force["S" + k] + force["D" + k] if k != "SS" else force["D" + k] for k in ("SS", "SD", "DS", "DD")})
        if carry is not None:
            store(element, [spread({k: a[k] + b[k] for k in a}) for a, b in zip(carry, lower)])
        carry = upper
        low = high


def fold(array):
    return jnp.sum(jnp.sum(array, axis=0), axis=0, keepdims=True)


def kernel(tiles, loads, u_ref, density_ref, blocks_ref, fixed_ref, nodes_ref, forces_ref,
           out_ref, sens_ref,
           ext, inv_s, free_s, force_s, r_s, z_s, q_s, w_s, aw_s, red, red2, en, parts, final,
           halo_send, halo_recv, red_send, red_recv, red2_send, red2_recv,
           part_send, part_recv, final_send, final_recv):
    me = lax.axis_index("tile")
    mine = lax.axis_index("load")
    planes, ny, nz = density_ref.shape
    tile_peers = [lax.rem(me + k, tiles) for k in range(1, tiles)]
    load_peers = [lax.rem(mine + k, loads) for k in range(1, loads)]

    barrier = pltpu.get_barrier_semaphore()
    for peer in tile_peers:
        pl.semaphore_signal(barrier, inc=1, device_id=(mine, peer), device_id_type=MESH)
    for peer in load_peers:
        pl.semaphore_signal(barrier, inc=1, device_id=(peer, me), device_id_type=MESH)

    widen = (lax.broadcasted_iota(jnp.int32, (nz // BLOCK, nz), 1) // BLOCK
             == lax.broadcasted_iota(jnp.int32, (nz // BLOCK, nz), 0)).astype(jnp.float32)
    rows = lax.broadcasted_iota(jnp.int32, (ny, nz // BLOCK), 0) // BLOCK
    masks = []
    for bx in range(planes // BLOCK):
        tall = jnp.zeros((ny, nz // BLOCK), jnp.float32)
        for by in range(ny // BLOCK):
            marked = (blocks_ref[bx, by:by + 1, :] == 1).astype(jnp.float32)
            tall = jnp.where(rows == by, marked, tall)
        masks.append(jnp.dot(tall, widen, preferred_element_type=jnp.float32))
    for plane in range(planes):
        dens = density_ref[plane]
        held = (fixed_ref[plane] != 0).astype(jnp.float32)
        ext[3, DEEP + plane] = dens * dens * dens * masks[plane // BLOCK]
        ext[4, DEEP + plane] = held
        for c in range(3):
            ext[c, DEEP + plane] = u_ref[0, c, plane] * (1.0 - held)

    pl.semaphore_wait(barrier, tiles + loads - 2)

    def halo(way):
        if way == 0:
            return pltpu.make_async_remote_copy(
                src_ref=ext.at[:, DEEP:2 * DEEP], dst_ref=ext.at[:, planes + DEEP:planes + 2 * DEEP],
                send_sem=halo_send.at[0], recv_sem=halo_recv.at[0],
                device_id=(mine, jnp.maximum(me - 1, 0)), device_id_type=MESH)
        return pltpu.make_async_remote_copy(
            src_ref=ext.at[:, planes:planes + DEEP], dst_ref=ext.at[:, 0:DEEP],
            send_sem=halo_send.at[1], recv_sem=halo_recv.at[1],
            device_id=(mine, jnp.minimum(me + 1, tiles - 1)), device_id_type=MESH)

    @pl.when(me > 0)
    def _():
        halo(0).start()

    @pl.when(me < tiles - 1)
    def _():
        halo(1).start()

    wide = planes + 4
    base = (me * planes - 2) * ny
    ids = nodes_ref[...]
    row_of = ids // nz - base
    lane_of = lax.rem(ids, nz)
    points = ids.shape[1]
    pick_row = (lax.broadcasted_iota(jnp.int32, (wide * ny, points), 0) == row_of).astype(jnp.float32)
    pick_lane = (lax.broadcasted_iota(jnp.int32, (nz, points), 0) == lane_of).astype(jnp.float32)
    for c in range(3):
        placed = pick_lane * forces_ref[0, c:c + 1, :]
        force_s[c] = lax.dot_general(pick_row, placed, (((1,), (1,)), ((), ())),
                                     precision=lax.Precision.HIGHEST,
                                     preferred_element_type=jnp.float32).reshape(wide, ny, nz)

    @pl.when(me == 0)
    def _():
        ext[:, 0:DEEP] = jnp.zeros((5, DEEP, ny, nz), jnp.float32)

    @pl.when(me == tiles - 1)
    def _():
        ext[0:4, planes + DEEP:planes + 2 * DEEP] = jnp.zeros((4, DEEP, ny, nz), jnp.float32)
        ext[4:5, planes + DEEP:planes + 2 * DEEP] = jnp.ones((1, DEEP, ny, nz), jnp.float32)

    @pl.when(me < tiles - 1)
    def _():
        halo(0).wait_recv()

    @pl.when(me > 0)
    def _():
        halo(1).wait_recv()

    def summed(plane):
        weight = ext[3, plane:plane + 1]
        part = weight + down(weight, 2)
        return part + down(part, 1)

    before = summed(0)
    for node in range(wide):
        after = summed(node + 1)
        diagonal = DIAG * (before + after)
        free = jnp.where((ext[4, node + 1:node + 2] == 0.0) & (diagonal > 0.0), 1.0, 0.0)
        free_s[node:node + 1] = free
        inv_s[node:node + 1] = free / (diagonal + 1.0 - free)
        before = after

    def store_residual(node, image):
        at = node - 1
        free, inv = free_s[at:at + 1], inv_s[at:at + 1]
        for c in range(3):
            left = free * (force_s[c, at:at + 1] - image[c])
            r_s[c, at:at + 1] = left
            z_s[c, at:at + 1] = inv * left

    stiffness(lambda i: [ext[c, i:i + 1] for c in range(3)],
              lambda e: ext[3, e:e + 1], store_residual, planes + 5)

    def store_image(node, image):
        at = node - 1
        free, inv = free_s[node:node + 1], inv_s[node:node + 1]
        for c in range(3):
            q = free * image[c]
            q_s[c, at:at + 1] = q
            w_s[c, at:at + 1] = inv * q

    stiffness(lambda i: [z_s[c, i:i + 1] for c in range(3)],
              lambda e: ext[3, e + 1:e + 2], store_image, planes + 3)

    def gather(slots, send, recv, values):
        row = lax.broadcasted_iota(jnp.int32, (8, nz), 0)
        block = jnp.zeros((8, nz), jnp.float32)
        for index, value in enumerate(values):
            block = jnp.where(row == index, value, block)
        slots[me] = block
        copies = []
        for k, peer in enumerate(tile_peers):
            copy = pltpu.make_async_remote_copy(
                src_ref=slots.at[me], dst_ref=slots.at[me],
                send_sem=send.at[k], recv_sem=recv.at[k],
                device_id=(mine, peer), device_id_type=MESH)
            copy.start()
            copies.append(copy)
        return copies

    def total(slots, copies):
        for copy in copies:
            copy.wait_recv()
        block = slots[0]
        for t in range(1, tiles):
            block = block + slots[t]
        return jnp.sum(block, axis=1, keepdims=True)

    def dot(pairs):
        return fold(sum(a * b for a, b in pairs))

    own = [(r_s[c, 2:2 + planes], z_s[c, 2:2 + planes], q_s[c, 1:1 + planes]) for c in range(3)]
    copies1 = gather(red, red_send, red_recv,
                     [dot([(r, z) for r, z, q in own]), dot([(z, q) for r, z, q in own])])

    def store_second(node, image):
        at = node - 1
        free = free_s[node + 1:node + 2]
        for c in range(3):
            aw_s[c, at:at + 1] = free * image[c]

    stiffness(lambda i: [w_s[c, i:i + 1] for c in range(3)],
              lambda e: ext[3, e + 2:e + 3], store_second, planes + 1)

    sums = total(red, copies1)
    inner, curve = sums[0:1, :], sums[1:2, :]
    alpha = inner / curve
    g_parts, s_parts, t_parts = [], [], []
    for c in range(3):
        q = q_s[c, 1:1 + planes]
        r1 = r_s[c, 2:2 + planes] - alpha[None] * q
        z1 = z_s[c, 2:2 + planes] - alpha[None] * w_s[c, 1:1 + planes]
        g_parts.append((r1, z1))
        s_parts.append((z1, q - alpha[None] * aw_s[c]))
        t_parts.append((z1, q))
    copies2 = gather(red2, red2_send, red2_recv, [dot(g_parts), dot(s_parts), dot(t_parts)])
    sums = total(red2, copies2)
    inner2, second, cross = sums[0:1, :], sums[1:2, :], sums[2:3, :]
    beta = inner2 / inner
    alpha2 = inner2 / (second + 2.0 * beta * cross + beta * beta * curve)
    by_z = (alpha + alpha2 * (1.0 + beta))[None]
    by_w = (alpha2 * alpha)[None]

    low = None
    for plane in range(planes + 1):
        fields = []
        free = free_s[plane + 2:plane + 3]
        for c in range(3):
            moved = free * ext[c, DEEP + plane:DEEP + plane + 1]
            moved = moved + by_z * z_s[c, plane + 2:plane + 3] - by_w * w_s[c, plane + 1:plane + 2]
            if plane < planes:
                out_ref[0, c, plane:plane + 1] = moved
            fields.append(moved)
        high = [flat_modes(field) for field in fields]
        if plane > 0:
            en[(plane - 1) * ny:plane * ny, :] = mode_energy(cube_modes(low, high))[0]
        low = high

    share = planes * ny // loads
    copies3 = []
    for k, peer in enumerate(load_peers):
        copy = pltpu.make_async_remote_copy(
            src_ref=en.at[pl.ds(pl.multiple_of(peer * share, 8), share)], dst_ref=parts.at[k],
            send_sem=part_send.at[k], recv_sem=part_recv.at[k],
            device_id=(peer, me), device_id_type=MESH)
        copy.start()
        copies3.append(copy)
    here = pl.ds(pl.multiple_of(mine * share, 8), share)
    energy = en[here]
    for k, copy in enumerate(copies3):
        copy.wait_recv()
        energy = energy + parts[k]
    final[here] = energy
    copies4 = []
    for k, peer in enumerate(load_peers):
        copy = pltpu.make_async_remote_copy(
            src_ref=final.at[here], dst_ref=final.at[here],
            send_sem=final_send.at[k], recv_sem=final_recv.at[k],
            device_id=(peer, me), device_id_type=MESH)
        copy.start()
        copies4.append(copy)
    for copy in copies4:
        copy.wait_recv()
    for plane in range(planes):
        dens = density_ref[plane]
        sens_ref[plane] = (-3.0 / loads) * dens * dens * masks[plane // BLOCK] * final[plane * ny:(plane + 1) * ny, :]

    @pl.when(me > 0)
    def _():
        halo(0).wait_send()

    @pl.when(me < tiles - 1)
    def _():
        halo(1).wait_send()

    for copy in copies1 + copies2 + copies3 + copies4:
        copy.wait_send()


def shards(tiles, loads, u_prev, density, active_blocks, fixed_nodes, load_nodes, load_forces):
    planes, ny, nz = density.shape
    wide = planes + 4
    vmem = pl.BlockSpec(memory_space=pltpu.VMEM)
    dma = pltpu.SemaphoreType.DMA

    def field(count, *lead):
        return pltpu.VMEM((*lead, count, ny, nz), jnp.float32)

    share = planes * ny // loads
    return pl.pallas_call(
        functools.partial(kernel, tiles, loads),
        out_shape=(jax.ShapeDtypeStruct(u_prev.shape, jnp.float32),
                   jax.ShapeDtypeStruct(density.shape, jnp.float32)),
        in_specs=[vmem] * 6,
        out_specs=(vmem, vmem),
        scratch_shapes=[
            field(planes + 2 * DEEP, 5),
            field(wide), field(wide), field(wide, 3),
            field(wide, 3), field(wide, 3), field(planes + 2, 3), field(planes + 2, 3), field(planes, 3),
            pltpu.VMEM((tiles, 8, nz), jnp.float32), pltpu.VMEM((tiles, 8, nz), jnp.float32),
            pltpu.VMEM((planes * ny, nz), jnp.float32),
            pltpu.VMEM((loads - 1, share, nz), jnp.float32),
            pltpu.VMEM((planes * ny, nz), jnp.float32),
            dma((2,)), dma((2,)),
            dma((tiles - 1,)), dma((tiles - 1,)), dma((tiles - 1,)), dma((tiles - 1,)),
            dma((loads - 1,)), dma((loads - 1,)), dma((loads - 1,)), dma((loads - 1,)),
        ],
        compiler_params=pltpu.CompilerParams(
            collective_id=0, has_side_effects=True, vmem_limit_bytes=32 * 1024 * 1024),
    )(u_prev, density, active_blocks, fixed_nodes, load_nodes, load_forces)


def solution(mesh):
    in_specs = (
        P("load", None, "tile", None, None),
        P("tile", None, None),
        P("tile", None, None),
        P("tile", None, None),
        P("load", None),
        P("load", None, None),
    )
    out_specs = (P("load", None, "tile", None, None), P("tile", None, None))
    body = functools.partial(shards, mesh.shape["tile"], mesh.shape["load"])
    return jax.shard_map(body, mesh=mesh, in_specs=in_specs, out_specs=out_specs, check_vma=False)
```

time: 177 us -> 31.4 us (0.18)
  waiting for transfers between devices: 46.9 us -> 0 us
  blocking collectives: 42.3 us -> 0 us
  Pallas kernels: 0 us -> 25.9 us
  local copies, waits for them, and re-layouts: 26.7 us -> 4.62 us
  starting transfers between devices: 19.3 us -> 0 us
  between operations: 18.7 us -> 0.66 us
  other arithmetic: 13.2 us -> 0 us
  matrix products: 8.76 us -> 0 us
    psum x3 -> x0, blocking collectives: 42.3 us -> none  [the longest x2 26.9 us: residual_sum(): return lax.psum(jnp.sum(residual * precond), 'tile')]
    psum x1 -> x0, waiting for transfers between devices: 37 us -> none  [shards(): sensitivity = lax.psum(own_terms, 'load')]
    pallas_call x0 -> x1, Pallas kernels: none -> 25.9 us  [shards(): pl.pallas_call(functools.partial(kernel, tiles, loads), out_shape=(jax.Sh...]
    ppermute x8 -> x0, starting transfers between devices: 19.3 us -> none  [shifted(): return lax.ppermute(array, axis, pairs)]
    concatenate x8 -> x0, local copies, waits for them, and re-layouts: 15.2 us -> none  [stacked_corners(): return jnp.concatenate(pieces, axis=0)]
    ppermute x8 -> x0, waiting for transfers between devices: 9.9 us -> none  [shifted(): return lax.ppermute(array, axis, pairs)]
    dot_general x4 -> x0, matrix products: 8.76 us -> none  [element_forces(): jnp.dot(matrix, flat, precision=lax.Precision.HIGHEST, preferred_element_...]
    reshape x1 -> x0, local copies, waits for them, and re-layouts: 5.22 us -> none  [shards(): force_field = force_field.reshape(3, planes, size_y, size_z)]
  transfers between devices with their start and end apart: 9 -> 0, of which waited for: 7 -> 0; matrix products, arithmetic and copies ran while one was open for 7% -> 0% of each run, Pallas kernels for 0% -> 0%
where the time goes in v1:
time: 31.4 us; the launch traced here: 31.2 us
  Pallas kernels  25.9 us (82%)
  local copies, waits for them, and re-layouts  4.62 us (15%)
  between operations  0.66 us (2%)
    pallas_call x1, Pallas kernels, shards(): pl.pallas_call(functools.partial(kernel, tiles, loads), out_shape=(jax.Sh...  25.9 us
    unnamed x13, local copies, waits for them, and re-layouts  4.62 us

profile of v1, /device:TPU:0, one launch (start us, length us, event | category | flops | bytes accessed | tf_op | source)
XLA Modules:
  0.0 31.2 jit_solution(11126595273300037107)
XLA Ops:
  0.6 0.0 copy-start.4
  0.6 0.0 copy-start.3
  0.7 0.7 %copy.8.forces_ref = f32[1,3,32]{2,1,0:T(4,128)S(1)} copy(f32[1,3,32]{2,0,1:T(1,128)} %param.11) | data formatting | bytes 768 | tf_op args[5]
  1.3 0.0 copy-done.4
  1.3 0.0 copy-done.3
  1.3 0.0 copy-start
  1.4 0.9 %copy-done = f32[1,3,8,16,128]{4,3,2,1,0:T(8,128)S(1)} copy-done((f32[1,3,8,16,128]{4,3,2,1,0:T(8,128)S(1)}, f32[1,3,8,16,128]{4,3,2,1,0:T(8,128)}, u32[]{:S(2)}) %copy-start) | copy-done | bytes 196632
  2.3 0.0 copy-start.1
  2.3 0.8 %copy-done.1 = f32[8,16,128]{2,1,0:T(8,128)S(1)} copy-done((f32[8,16,128]{2,1,0:T(8,128)S(1)}, f32[8,16,128]{2,1,0:T(8,128)}, u32[]{:S(2)}) %copy-start.1) | copy-done | bytes 65560
  3.1 0.0 copy-start.2
  3.1 0.8 %copy-done.2 = s32[8,16,128]{2,1,0:T(8,128)S(1)} copy-done((s32[8,16,128]{2,1,0:T(8,128)S(1)}, s32[8,16,128]{2,1,0:T(8,128)}, u32[]{:S(2)}) %copy-start.2) | copy-done | bytes 65560
  4.0 25.9 %shard_map.77 = (f32[1,3,8,16,128]{4,3,2,1,0:T(8,128)S(1)}, f32[8,16,128]{2,1,0:T(8,128)S(1)}) custom-call(f32[1,3,8,16,128]{4,3,2,1,0:T(8,128)S(1)} %copy-done, f32[8,16,128]{2,1,0:T(8,128)S(1)} %copy-done.1, s32[1,2,16]{2,1,0:T(2,128)S(1)} %copy-done.3, s32[8,16,128]{2,1,0:T(8,128)S(1)} %copy-done.2, s32[1,32]{1,0:T(1,128)S(1)} %copy-done.4, ...), custom_call_target="tpu_custom_call" | custom-call | tf_op jit(solution)/shard_map/pallas_call | solution.py:377
  29.9 0.7 %copy.11 = f32[1,3,8,16,128]{4,3,2,1,0:T(8,128)} copy(f32[1,3,8,16,128]{4,3,2,1,0:T(8,128)S(1)} %get-tuple-element.4) | data formatting | bytes 393216
  30.5 0.6 %copy.12 = f32[8,16,128]{2,1,0:T(8,128)} copy(f32[8,16,128]{2,1,0:T(8,128)S(1)} %get-tuple-element.5) | data formatting | bytes 131072
Async XLA Ops:
  0.6 0.7 %copy-start.4 = (s32[1,32]{1,0:T(1,128)S(1)}, s32[1,32]{1,0:T(1,128)}, u32[]{:S(2)}) copy-start(s32[1,32]{1,0:T(1,128)} %nodes_ref.1) | copy-start | bytes 388
  0.6 0.7 %copy-start.3 = (s32[1,2,16]{2,1,0:T(2,128)S(1)}, s32[1,2,16]{2,1,0:T(2,128)}, u32[]{:S(2)}) copy-start(s32[1,2,16]{2,1,0:T(2,128)} %blocks_ref.1) | copy-start | bytes 388
  1.3 0.9 %copy-start = (f32[1,3,8,16,128]{4,3,2,1,0:T(8,128)S(1)}, f32[1,3,8,16,128]{4,3,2,1,0:T(8,128)}, u32[]{:S(2)}) copy-start(f32[1,3,8,16,128]{4,3,2,1,0:T(8,128)} %u_ref.1) | copy-start | bytes 589828
  2.3 0.8 %copy-start.1 = (f32[8,16,128]{2,1,0:T(8,128)S(1)}, f32[8,16,128]{2,1,0:T(8,128)}, u32[]{:S(2)}) copy-start(f32[8,16,128]{2,1,0:T(8,128)} %density_ref.1) | copy-start | bytes 196612
  3.1 0.8 %copy-start.2 = (s32[8,16,128]{2,1,0:T(8,128)S(1)}, s32[8,16,128]{2,1,0:T(8,128)}, u32[]{:S(2)}) copy-start(s32[8,16,128]{2,1,0:T(8,128)} %fixed_ref.1) | copy-start | bytes 196612

commit v2 on v1

--- a/solution.py
+++ b/solution.py
@@ -126,10 +126,11 @@
     return jnp.sum(jnp.sum(array, axis=0), axis=0, keepdims=True)
 
 
-def kernel(tiles, loads, u_ref, density_ref, blocks_ref, fixed_ref, nodes_ref, forces_ref,
-           out_ref, sens_ref,
-           ext, inv_s, free_s, force_s, r_s, z_s, q_s, w_s, aw_s, red, red2, en, parts, final,
-           halo_send, halo_recv, red_send, red_recv, red2_send, red2_recv,
+def kernel(tiles, loads, u_in, density_in, blocks_in, fixed_in, nodes_in, forces_in,
+           out_hbm, sens_ref,
+           out_ref, out_sem,
+           u_ref, density_ref, blocks_ref, fixed_ref, nodes_ref, forces_ref, in_sem, ext, inv_s, free_s, force_s, r_s, z_s, q_s, w_s, aw_s, move_s, red, en, parts, final,
+           halo_send, halo_recv, red_send, red_recv,
            part_send, part_recv, final_send, final_recv):
     me = lax.axis_index("tile")
     mine = lax.axis_index("load")
@@ -137,6 +138,13 @@
     tile_peers = [lax.rem(me + k, tiles) for k in range(1, tiles)]
     load_peers = [lax.rem(mine + k, loads) for k in range(1, loads)]
 
+    arrivals = []
+    for index, (source, target) in enumerate((
+            (density_in, density_ref), (fixed_in, fixed_ref), (blocks_in, blocks_ref),
+            (u_in, u_ref), (nodes_in, nodes_ref), (forces_in, forces_ref))):
+        arrival = pltpu.make_async_copy(source, target, in_sem.at[index])
+        arrival.start()
+        arrivals.append(arrival)
     barrier = pltpu.get_barrier_semaphore()
     for peer in tile_peers:
         pl.semaphore_signal(barrier, inc=1, device_id=(mine, peer), device_id_type=MESH)
@@ -146,6 +154,8 @@
     widen = (lax.broadcasted_iota(jnp.int32, (nz // BLOCK, nz), 1) // BLOCK
              == lax.broadcasted_iota(jnp.int32, (nz // BLOCK, nz), 0)).astype(jnp.float32)
     rows = lax.broadcasted_iota(jnp.int32, (ny, nz // BLOCK), 0) // BLOCK
+    for arrival in arrivals:
+        arrival.wait()
     masks = []
     for bx in range(planes // BLOCK):
         tall = jnp.zeros((ny, nz // BLOCK), jnp.float32)
@@ -191,7 +201,7 @@
     pick_row = (lax.broadcasted_iota(jnp.int32, (wide * ny, points), 0) == row_of).astype(jnp.float32)
     pick_lane = (lax.broadcasted_iota(jnp.int32, (nz, points), 0) == lane_of).astype(jnp.float32)
     for c in range(3):
-        placed = pick_lane * forces_ref[0, c:c + 1, :]
+        placed = pick_lane * forces_ref[c]
         force_s[c] = lax.dot_general(pick_row, placed, (((1,), (1,)), ((), ())),
                                      precision=lax.Precision.HIGHEST,
                                      preferred_element_type=jnp.float32).reshape(wide, ny, nz)
@@ -277,9 +287,6 @@
         return fold(sum(a * b for a, b in pairs))
 
     own = [(r_s[c, 2:2 + planes], z_s[c, 2:2 + planes], q_s[c, 1:1 + planes]) for c in range(3)]
-    copies1 = gather(red, red_send, red_recv,
-                     [dot([(r, z) for r, z, q in own]), dot([(z, q) for r, z, q in own])])
-
     def store_second(node, image):
         at = node - 1
         free = free_s[node + 1:node + 2]
@@ -289,49 +296,60 @@
     stiffness(lambda i: [w_s[c, i:i + 1] for c in range(3)],
               lambda e: ext[3, e + 2:e + 3], store_second, planes + 1)
 
+    seconds = [(w_s[c, 1:1 + planes], q_s[c, 1:1 + planes], aw_s[c]) for c in range(3)]
+    copies1 = gather(red, red_send, red_recv,
+                     [dot([(r, z) for r, z, q in own]), dot([(z, q) for r, z, q in own]),
+                      dot([(w, q) for w, q, image in seconds]), dot([(w, image) for w, q, image in seconds])])
     sums = total(red, copies1)
-    inner, curve = sums[0:1, :], sums[1:2, :]
+    inner, curve, square, bent = sums[0:1, :], sums[1:2, :], sums[2:3, :], sums[3:4, :]
     alpha = inner / curve
-    g_parts, s_parts, t_parts = [], [], []
-    for c in range(3):
-        q = q_s[c, 1:1 + planes]
-        r1 = r_s[c, 2:2 + planes] - alpha[None] * q
-        z1 = z_s[c, 2:2 + planes] - alpha[None] * w_s[c, 1:1 + planes]
-        g_parts.append((r1, z1))
-        s_parts.append((z1, q - alpha[None] * aw_s[c]))
-        t_parts.append((z1, q))
-    copies2 = gather(red2, red2_send, red2_recv, [dot(g_parts), dot(s_parts), dot(t_parts)])
-    sums = total(red2, copies2)
-    inner2, second, cross = sums[0:1, :], sums[1:2, :], sums[2:3, :]
+    inner2 = inner - 2.0 * alpha * curve + alpha * alpha * square
     beta = inner2 / inner
+    cross = curve - alpha * square
+    second = curve - 2.0 * alpha * square + alpha * alpha * bent
     alpha2 = inner2 / (second + 2.0 * beta * cross + beta * beta * curve)
     by_z = (alpha + alpha2 * (1.0 + beta))[None]
     by_w = (alpha2 * alpha)[None]
 
-    low = None
     for plane in range(planes + 1):
-        fields = []
         free = free_s[plane + 2:plane + 3]
         for c in range(3):
             moved = free * ext[c, DEEP + plane:DEEP + plane + 1]
             moved = moved + by_z * z_s[c, plane + 2:plane + 3] - by_w * w_s[c, plane + 1:plane + 2]
             if plane < planes:
                 out_ref[0, c, plane:plane + 1] = moved
-            fields.append(moved)
-        high = [flat_modes(field) for field in fields]
-        if plane > 0:
-            en[(plane - 1) * ny:plane * ny, :] = mode_energy(cube_modes(low, high))[0]
-        low = high
+            move_s[c, plane:plane + 1] = moved
+
+    leaving = pltpu.make_async_copy(out_ref, out_hbm, out_sem)
+    leaving.start()
+
+    def energies(start, count):
+        low = None
+        for step in range(count + 1):
+            high = [flat_modes(move_s[c, pl.ds(start + step, 1)]) for c in range(3)]
+            if step > 0:
+                spot = (start + step - 1) * ny
+                if not isinstance(spot, int):
+                    spot = pl.multiple_of(spot, 8)
+                en[pl.ds(spot, ny), :] = mode_energy(cube_modes(low, high))[0]
+            low = high
 
     share = planes * ny // loads
+    by_share = share % ny == 0
+    if not by_share:
+        energies(0, planes)
     copies3 = []
     for k, peer in enumerate(load_peers):
+        if by_share:
+            energies(peer * (share // ny), share // ny)
         copy = pltpu.make_async_remote_copy(
             src_ref=en.at[pl.ds(pl.multiple_of(peer * share, 8), share)], dst_ref=parts.at[k],
             send_sem=part_send.at[k], recv_sem=part_recv.at[k],
             device_id=(peer, me), device_id_type=MESH)
         copy.start()
         copies3.append(copy)
+    if by_share:
+        energies(mine * (share // ny), share // ny)
     here = pl.ds(pl.multiple_of(mine * share, 8), share)
     energy = en[here]
     for k, copy in enumerate(copies3):
@@ -360,7 +378,8 @@
     def _():
         halo(1).wait_send()
 
-    for copy in copies1 + copies2 + copies3 + copies4:
+    leaving.wait()
+    for copy in copies1 + copies3 + copies4:
         copy.wait_send()
 
 
@@ -378,23 +397,28 @@
         functools.partial(kernel, tiles, loads),
         out_shape=(jax.ShapeDtypeStruct(u_prev.shape, jnp.float32),
                    jax.ShapeDtypeStruct(density.shape, jnp.float32)),
-        in_specs=[vmem] * 6,
-        out_specs=(vmem, vmem),
+        in_specs=[pl.BlockSpec(memory_space=pltpu.HBM)] * 6,
+        out_specs=(pl.BlockSpec(memory_space=pltpu.HBM), vmem),
         scratch_shapes=[
+            pltpu.VMEM(u_prev.shape, jnp.float32), dma(()),
+            pltpu.VMEM(u_prev.shape, jnp.float32), pltpu.VMEM(density.shape, jnp.float32),
+            pltpu.VMEM(active_blocks.shape, jnp.int32), pltpu.VMEM(fixed_nodes.shape, jnp.int32),
+            pltpu.VMEM(load_nodes.shape, jnp.int32), pltpu.VMEM((3, 1, load_forces.shape[2]), jnp.float32),
+            dma((6,)),
             field(planes + 2 * DEEP, 5),
             field(wide), field(wide), field(wide, 3),
-            field(wide, 3), field(wide, 3), field(planes + 2, 3), field(planes + 2, 3), field(planes, 3),
-            pltpu.VMEM((tiles, 8, nz), jnp.float32), pltpu.VMEM((tiles, 8, nz), jnp.float32),
+            field(wide, 3), field(wide, 3), field(planes + 2, 3), field(planes + 2, 3), field(planes, 3), field(planes + 1, 3),
+            pltpu.VMEM((tiles, 8, nz), jnp.float32),
             pltpu.VMEM((planes * ny, nz), jnp.float32),
             pltpu.VMEM((loads - 1, share, nz), jnp.float32),
             pltpu.VMEM((planes * ny, nz), jnp.float32),
             dma((2,)), dma((2,)),
-            dma((tiles - 1,)), dma((tiles - 1,)), dma((tiles - 1,)), dma((tiles - 1,)),
+            dma((tiles - 1,)), dma((tiles - 1,)),
             dma((loads - 1,)), dma((loads - 1,)), dma((loads - 1,)), dma((loads - 1,)),
         ],
         compiler_params=pltpu.CompilerParams(
-            collective_id=0, has_side_effects=True, vmem_limit_bytes=32 * 1024 * 1024),
-    )(u_prev, density, active_blocks, fixed_nodes, load_nodes, load_forces)
+            collective_id=0, has_side_effects=True, vmem_limit_bytes=58 * 1024 * 1024),
+    )(u_prev, density, active_blocks, fixed_nodes, load_nodes, load_forces.transpose(1, 0, 2))
 
 
 def solution(mesh):

time: 31.4 us -> 26.5 us (0.84)
  Pallas kernels: 25.9 us -> 23.4 us
  local copies, waits for them, and re-layouts: 4.62 us -> 2.28 us
    pallas_call x1, Pallas kernels: 25.9 us -> 23.4 us  [shards(): pl.pallas_call(functools.partial(kernel, tiles, loads), out_shape=(jax.Sh...]
    unnamed x13 -> x4, local copies, waits for them, and re-layouts: 4.62 us -> 2.28 us
where the time goes in v2:
time: 26.5 us; the launch traced here: 26.3 us
  Pallas kernels  23.4 us (88%)
  local copies, waits for them, and re-layouts  2.28 us (9%)
  between operations  0.65 us (2%)
    pallas_call x1, Pallas kernels, shards(): pl.pallas_call(functools.partial(kernel, tiles, loads), out_shape=(jax.Sh...  23.4 us
    unnamed x4, local copies, waits for them, and re-layouts  2.28 us

profile of v2, /device:TPU:0, one launch (start us, length us, event | category | flops | bytes accessed | tf_op | source)
XLA Modules:
  0.0 26.3 jit_solution(10661449718945567644)
XLA Ops:
  0.6 23.4 %shard_map.77 = (f32[1,3,8,16,128]{4,3,2,1,0:T(8,128)}, f32[8,16,128]{2,1,0:T(8,128)}) custom-call(f32[1,3,8,16,128]{4,3,2,1,0:T(8,128)} %u_in.1, f32[8,16,128]{2,1,0:T(8,128)} %density_in.1, s32[1,2,16]{2,1,0:T(2,128)} %blocks_in.1, s32[8,16,128]{2,1,0:T(8,128)} %fixed_in.1, s32[1,32]{1,0:T(1,128)} %nodes_in.1, f32[3,1,32]{2,1,0:T(1,128)} %bitcast.1), custom_call_target="tpu_custom_call" | custom-call | tf_op jit(solution)/shard_map/pallas_call | solution.py:396
  24.0 0.0 copy-start
  24.0 1.6 %copy.10 = f32[1,3,8,16,128]{4,3,2,1,0:T(8,128)} copy(f32[1,3,8,16,128]{4,3,2,1,0:T(8,128)} %get-tuple-element.4) | data formatting | bytes 393216
  25.7 0.0 copy-done
  25.7 0.6 %copy.11 = f32[8,16,128]{2,1,0:T(8,128)} copy(f32[8,16,128]{2,1,0:T(8,128)S(1)} %copy-done) | data formatting | bytes 131072
Async XLA Ops:
  24.0 1.7 %copy-start = (f32[8,16,128]{2,1,0:T(8,128)S(1)}, f32[8,16,128]{2,1,0:T(8,128)}, u32[]{:S(2)}) copy-start(f32[8,16,128]{2,1,0:T(8,128)} %get-tuple-element.5) | copy-start | bytes 196612

commit v3 on v2

--- a/solution.py
+++ b/solution.py
@@ -127,8 +127,7 @@
 
 
 def kernel(tiles, loads, u_in, density_in, blocks_in, fixed_in, nodes_in, forces_in,
-           out_hbm, sens_ref,
-           out_ref, out_sem,
+           out_ref, sens_ref,
            u_ref, density_ref, blocks_ref, fixed_ref, nodes_ref, forces_ref, in_sem, ext, inv_s, free_s, force_s, r_s, z_s, q_s, w_s, aw_s, move_s, red, en, parts, final,
            halo_send, halo_recv, red_send, red_recv,
            part_send, part_recv, final_send, final_recv):
@@ -206,47 +205,56 @@
                                      precision=lax.Precision.HIGHEST,
                                      preferred_element_type=jnp.float32).reshape(wide, ny, nz)
 
-    @pl.when(me == 0)
-    def _():
-        ext[:, 0:DEEP] = jnp.zeros((5, DEEP, ny, nz), jnp.float32)
-
-    @pl.when(me == tiles - 1)
-    def _():
-        ext[0:4, planes + DEEP:planes + 2 * DEEP] = jnp.zeros((4, DEEP, ny, nz), jnp.float32)
-        ext[4:5, planes + DEEP:planes + 2 * DEEP] = jnp.ones((1, DEEP, ny, nz), jnp.float32)
-
-    @pl.when(me < tiles - 1)
-    def _():
-        halo(0).wait_recv()
-
-    @pl.when(me > 0)
-    def _():
-        halo(1).wait_recv()
-
     def summed(plane):
         weight = ext[3, plane:plane + 1]
         part = weight + down(weight, 2)
         return part + down(part, 1)
 
-    before = summed(0)
-    for node in range(wide):
-        after = summed(node + 1)
-        diagonal = DIAG * (before + after)
-        free = jnp.where((ext[4, node + 1:node + 2] == 0.0) & (diagonal > 0.0), 1.0, 0.0)
-        free_s[node:node + 1] = free
-        inv_s[node:node + 1] = free / (diagonal + 1.0 - free)
-        before = after
-
-    def store_residual(node, image):
-        at = node - 1
-        free, inv = free_s[at:at + 1], inv_s[at:at + 1]
-        for c in range(3):
-            left = free * (force_s[c, at:at + 1] - image[c])
-            r_s[c, at:at + 1] = left
-            z_s[c, at:at + 1] = inv * left
-
-    stiffness(lambda i: [ext[c, i:i + 1] for c in range(3)],
-              lambda e: ext[3, e:e + 1], store_residual, planes + 5)
+    def masks_of(first, last):
+        before = summed(first)
+        for node in range(first, last):
+            after = summed(node + 1)
+            diagonal = DIAG * (before + after)
+            free = jnp.where((ext[4, node + 1:node + 2] == 0.0) & (diagonal > 0.0), 1.0, 0.0)
+            free_s[node:node + 1] = free
+            inv_s[node:node + 1] = free / (diagonal + 1.0 - free)
+            before = after
+
+    def residual(first, last):
+        masks_of(first, last)
+
+        def store_residual(node, image):
+            at = node + first - 1
+            free, inv = free_s[at:at + 1], inv_s[at:at + 1]
+            for c in range(3):
+                left = free * (force_s[c, at:at + 1] - image[c])
+                r_s[c, at:at + 1] = left
+                z_s[c, at:at + 1] = inv * left
+
+        stiffness(lambda i: [ext[c, first + i:first + i + 1] for c in range(3)],
+                  lambda e: ext[3, first + e:first + e + 1], store_residual, last - first + 1)
+
+    residual(3, planes + 1)
+
+    @pl.when(me == 0)
+    def _():
+        ext[:, 0:DEEP] = jnp.zeros((5, DEEP, ny, nz), jnp.float32)
+
+    @pl.when(me == tiles - 1)
+    def _():
+        ext[0:4, planes + DEEP:planes + 2 * DEEP] = jnp.zeros((4, DEEP, ny, nz), jnp.float32)
+        ext[4:5, planes + DEEP:planes + 2 * DEEP] = jnp.ones((1, DEEP, ny, nz), jnp.float32)
+
+    @pl.when(me < tiles - 1)
+    def _():
+        halo(0).wait_recv()
+
+    @pl.when(me > 0)
+    def _():
+        halo(1).wait_recv()
+
+    residual(0, 3)
+    residual(planes + 1, wide)
 
     def store_image(node, image):
         at = node - 1
@@ -319,9 +327,6 @@
             if plane < planes:
                 out_ref[0, c, plane:plane + 1] = moved
             move_s[c, plane:plane + 1] = moved
-
-    leaving = pltpu.make_async_copy(out_ref, out_hbm, out_sem)
-    leaving.start()
 
     def energies(start, count):
         low = None
@@ -378,7 +383,6 @@
     def _():
         halo(1).wait_send()
 
-    leaving.wait()
     for copy in copies1 + copies3 + copies4:
         copy.wait_send()
 
@@ -398,9 +402,8 @@
         out_shape=(jax.ShapeDtypeStruct(u_prev.shape, jnp.float32),
                    jax.ShapeDtypeStruct(density.shape, jnp.float32)),
         in_specs=[pl.BlockSpec(memory_space=pltpu.HBM)] * 6,
-        out_specs=(pl.BlockSpec(memory_space=pltpu.HBM), vmem),
+        out_specs=(vmem, vmem),
         scratch_shapes=[
-            pltpu.VMEM(u_prev.shape, jnp.float32), dma(()),
             pltpu.VMEM(u_prev.shape, jnp.float32), pltpu.VMEM(density.shape, jnp.float32),
             pltpu.VMEM(active_blocks.shape, jnp.int32), pltpu.VMEM(fixed_nodes.shape, jnp.int32),
             pltpu.VMEM(load_nodes.shape, jnp.int32), pltpu.VMEM((3, 1, load_forces.shape[2]), jnp.float32),
@@ -417,8 +420,9 @@
             dma((loads - 1,)), dma((loads - 1,)), dma((loads - 1,)), dma((loads - 1,)),
         ],
         compiler_params=pltpu.CompilerParams(
-            collective_id=0, has_side_effects=True, vmem_limit_bytes=58 * 1024 * 1024),
-    )(u_prev, density, active_blocks, fixed_nodes, load_nodes, load_forces.transpose(1, 0, 2))
+            collective_id=0, has_side_effects=True, vmem_limit_bytes=32 * 1024 * 1024),
+    )(*(pltpu.with_memory_space_constraint(array, pltpu.HBM) for array in (
+        u_prev, density, active_blocks, fixed_nodes, load_nodes, load_forces.transpose(1, 0, 2))))
 
 
 def solution(mesh):

time: 26.5 us -> 24.2 us (0.913)
  Pallas kernels: 23.4 us -> 22.1 us
  local copies, waits for them, and re-layouts: 2.28 us -> 1.31 us
    pallas_call x1, Pallas kernels: 23.4 us -> 22.1 us  [shards(): pl.pallas_call(functools.partial(kernel, tiles, loads), out_shape=(jax.Sh...]
    unnamed x4 -> x2, local copies, waits for them, and re-layouts: 2.28 us -> 1.31 us
where the time goes in v3:
time: 24.2 us; the launch traced here: 24 us
  Pallas kernels  22.1 us (91%)
  local copies, waits for them, and re-layouts  1.31 us (5%)
  between operations  0.64 us (3%)
    pallas_call x1, Pallas kernels, shards(): pl.pallas_call(functools.partial(kernel, tiles, loads), out_shape=(jax.Sh...  22.1 us
    unnamed x2, local copies, waits for them, and re-layouts  1.31 us

profile of v3, /device:TPU:0, one launch (start us, length us, event | category | flops | bytes accessed | tf_op | source)
XLA Modules:
  0.0 24.0 jit_solution(6784230346725651995)
XLA Ops:
  0.6 22.1 %shard_map.77 = (f32[1,3,8,16,128]{4,3,2,1,0:T(8,128)S(1)}, f32[8,16,128]{2,1,0:T(8,128)S(1)}) custom-call(f32[1,3,8,16,128]{4,3,2,1,0:T(8,128)} %u_in.1, f32[8,16,128]{2,1,0:T(8,128)} %density_in.1, s32[1,2,16]{2,1,0:T(2,128)} %blocks_in.1, s32[8,16,128]{2,1,0:T(8,128)} %fixed_in.1, s32[1,32]{1,0:T(1,128)} %nodes_in.1, f32[3,1,32]{2,1,0:T(1,128)} %bitcast.1), custom_call_target="tpu_custom_call" | custom-call | tf_op jit(solution)/shard_map/pallas_call | solution.py:400
  22.7 0.7 %copy.10 = f32[1,3,8,16,128]{4,3,2,1,0:T(8,128)} copy(f32[1,3,8,16,128]{4,3,2,1,0:T(8,128)S(1)} %get-tuple-element.4) | data formatting | bytes 393216
  23.4 0.6 %copy.11 = f32[8,16,128]{2,1,0:T(8,128)} copy(f32[8,16,128]{2,1,0:T(8,128)S(1)} %get-tuple-element.5) | data formatting | bytes 131072
